TPU v7x, 128 devices: a whole 4x4x4 slice. The times are simulated.
128 devices in a mesh: doc: 8 (over y, x_hi), cent: 16 (over z, x_lo, core).
Axes of the slice: x: 4 (x_hi: 2, x_lo: 2; x = x_hi * 2 + x_lo), y: 4, z: 4, core: 2. Of those that a mesh axis runs over, the one named last changes fastest.
Arguments:
- embeddings: float32 [65536, 1024], P(('doc', 'cent'))
- centroids: float32 [16384, 1024], P('cent')
- cluster: int32 [65536], P(('doc', 'cent')), may hold values from 0 to 16383, as said below
- slot: int32 [65536], P(('doc', 'cent')), may hold values from 0 to 7, as said below
Outputs:
- soft_cost: float32 [65536], P(('doc', 'cent'))
- dup_sim: float32 [65536], P(('doc', 'cent'))
Inputs may be any that keep to these rules, and one draw needn't show every extreme that they name: Owner device of row r is cluster[r] // 128; some owner device receives rows from every device. `slot`: slots of the rows of one device that have the same owner device are distinct; in every draw some owner device takes 8 rows from every device.
All inputs are finite; a program needn't handle non-finite values.
Results may differ from a plain program's by a relative error of at most 0.0003.
Values may be sent and summed in bfloat16 or wider, within the bound.
No kernel may reach another device: no remote copies, remote signals or barrier semaphores. Data moves between devices by JAX's collectives and lax.ppermute only.
A program may use at most 192 MiB of HBM per device.

v0:
```python
import jax
import jax.numpy as jnp
from jax import lax
from jax.sharding import PartitionSpec as P

inverse_temp = 256.0


def unit_rows(values):
    total = jnp.sum(values * values, axis=1, keepdims=True)
    return (values * lax.rsqrt(total + 1e-06)).astype(jnp.bfloat16)


def inner_rows(left, right):
    return lax.dot_general(
        left, right, (((1,), (1,)), ((), ())), preferred_element_type=jnp.float32
    )


def block_terms(part, centre):
    score = inner_rows(part, centre) * inverse_temp
    high = jnp.max(score, axis=1)
    return (high, jnp.sum(jnp.exp(score - high[:, None]), axis=1))


def join_terms(first, second):
    high = jnp.maximum(first[0], second[0])
    return (high, second[1] * jnp.exp(second[0] - high))


def owner_best(rows, ids):
    total = rows.shape[0]
    block = min(512, total)
    col_pos = jnp.arange(total)

    def one_block(index):
        start = index * block
        part = lax.dynamic_slice_in_dim(rows, start, block, 0)
        part_ids = lax.dynamic_slice_in_dim(ids, start, block, 0)
        gram = inner_rows(part, rows)
        row_pos = start + jnp.arange(block)
        mask = (
            (part_ids[:, None] == ids[None, :])
            & (ids[None, :] >= 0.0)
            & (col_pos[None, :] < row_pos[:, None])
        )
        return jnp.max(jnp.where(mask, gram, jnp.float32(-1.0)), axis=1)

    return lax.map(one_block, jnp.arange(total // block)).reshape(total)


def per_device(embeddings, centroids, cluster, slot):
    row_count, width = embeddings.shape
    doc_count = lax.axis_size("doc")
    cent_count = lax.axis_size("cent")
    devices = doc_count * cent_count
    per_owner = centroids.shape[0] // doc_count
    capacity = 2 * row_count // devices
    unit = unit_rows(embeddings)
    centre = unit_rows(centroids)
    start_terms = (jnp.full((row_count,), -1e30, jnp.float32), jnp.zeros((row_count,), jnp.float32))
    high, total = join_terms(
        start_terms, block_terms(unit, lax.all_gather(centre, "cent", axis=0, tiled=True))
    )
    soft_cost = 1.0 - (high + jnp.log(total)) / inverse_temp
    owner = cluster // per_owner
    local = (cluster % per_owner).astype(jnp.bfloat16)
    target = owner * capacity + slot
    send_rows = jnp.zeros((devices * capacity, width), jnp.bfloat16).at[target].set(unit)
    send_ids = jnp.full((devices * capacity,), -1.0, jnp.bfloat16).at[target].set(local)
    got_rows, got_ids = (
        lax.all_to_all(
            send_rows.reshape(devices, capacity, width),
            ("doc", "cent"),
            split_axis=0,
            concat_axis=0,
            tiled=True,
        ),
        lax.all_to_all(
            send_ids.reshape(devices, capacity),
            ("doc", "cent"),
            split_axis=0,
            concat_axis=0,
            tiled=True,
        ),
    )
    best = owner_best(
        got_rows.reshape(devices * capacity, width),
        got_ids.reshape(devices * capacity).astype(jnp.float32),
    )
    returned = lax.all_to_all(
        best.reshape(devices, capacity), ("doc", "cent"), split_axis=0, concat_axis=0, tiled=True
    )
    dup_sim = returned.reshape(devices * capacity)[target]
    return (soft_cost, dup_sim)


def solution(mesh):
    return jax.shard_map(
        per_device,
        mesh=mesh,
        in_specs=(
            P(("doc", "cent"), None),
            P("cent", None),
            P(("doc", "cent")),
            P(("doc", "cent")),
        ),
        out_specs=(P(("doc", "cent")), P(("doc", "cent"))),
        check_vma=False,
    )
```

profile of v0, /device:TPU:1, one launch (start us, length us, event | category | flops | bytes accessed | tf_op | source)
XLA Modules:
  0.0 260.8 jit_solution(17680688221776090694)
XLA Ops:
  7.2 0.0 all-gather.2.cloned.1.call-start
  7.2 0.0 copy-start
  7.2 2.7 %multiply_reduce_fusion.1 = f32[1024]{0:T(1024)S(1)} fusion(f32[1024,1024]{1,0:T(8,128)} %param.7), kind=kLoop, calls=%fused_computation.14 | loop fusion | flops 2096128 | bytes 4198400 | tf_op jit(solution)/shard_map/reduce_sum | solution.py:10
  9.9 0.7 copy-done
  10.7 0.0 copy-start.3
  10.7 1.6 multiply_convert_fusion
  12.3 0.0 copy-start.2
  12.3 0.0 copy-start.1
  12.3 0.0 all-gather.2.cloned.1.call-update
  12.3 0.0 copy-done.3
  12.3 0.6 copy-done.2
  13.0 3.8 %scatter_custom_fusion = bf16[1024]{0:T(1024)(128)(2,1)S(1)} fusion(s32[512]{0:T(512)S(1)} %get-tuple-element.58, bf16[512]{0:T(512)(128)(2,1)S(1)} %get-tuple-element.57, bf16[]{:T(256)} %constant.72.clone.1), kind=kCustom, calls=%fused_computation.42 | custom fusion | bytes 2050 | tf_op jit(solution)/shard_map/scatter | solution.py:70
  16.7 0.8 all_to_all.20
  17.5 11.5 %all-to-all-start = ((bf16[128,1,8]{2,1,0:T(2,128)(2,1)}), bf16[128,1,8]{2,1,0:T(2,128)(2,1)S(1)}, u32[]{:S(2)}, u32[]{:S(2)}) async-start(bf16[128,1,8]{2,1,0:T(2,128)(2,1)} %all_to_all.20), calls=%async_computation | async-start | bytes 131072 | tf_op jit(solution)/shard_map/all_to_all | solution.py:79
  29.0 0.0 copy-done.1
  29.0 0.2 multiply_reduce_fusion.2
  29.2 4.2 %scatter_custom_fusion.1 = bf16[1024,1024]{1,0:T(8,128)(2,1)} fusion(s32[512]{0:T(512)S(1)} %get-tuple-element.58, bf16[]{:T(256)} %constant.65.clone.1, f32[512,1024]{1,0:T(8,128)S(1)} %copy-done.1, f32[512]{0:T(512)S(1)} %add_rsqrt_fusion.1), kind=kCustom, calls=%fused_computation.17 | custom fusion | flops 1048576 | bytes 4196354 | tf_op jit(solution)/shard_map/scatter | solution.py:69
  33.5 5.4 %all-to-all-done = bf16[128,1,8]{2,1,0:T(2,128)(2,1)S(1)} async-done(((bf16[128,1,8]{2,1,0:T(2,128)(2,1)}), bf16[128,1,8]{2,1,0:T(2,128)(2,1)S(1)}, u32[]{:S(2)}, u32[]{:S(2)}) %all-to-all-start) | async-done | bytes 2080 | tf_op jit(solution)/shard_map/all_to_all | solution.py:79
  38.8 5.3 %all-to-all-start.1 = ((bf16[128,8,1024]{2,1,0:T(8,128)(2,1)}), bf16[128,8,1024]{2,1,0:T(8,128)(2,1)}, u32[]{:S(2)}, u32[]{:S(2)}) async-start(bf16[128,8,1024]{2,1,0:T(8,128)(2,1)} %bitcast.13), calls=%async_computation.1 | async-start | bytes 4194304 | tf_op jit(solution)/shard_map/all_to_all | solution.py:72
  44.2 0.2 convert_reduce_fusion
  44.4 0.1 reshape.54
  44.5 52.5 %all-to-all-done.1 = bf16[128,8,1024]{2,1,0:T(8,128)(2,1)} async-done(((bf16[128,8,1024]{2,1,0:T(8,128)(2,1)}), bf16[128,8,1024]{2,1,0:T(8,128)(2,1)}, u32[]{:S(2)}, u32[]{:S(2)}) %all-to-all-start.1) | async-done | bytes 2097184 | tf_op jit(solution)/shard_map/all_to_all | solution.py:72
  97.0 10.0 %while.11 = (s32[]{:T(128)}, f32[2,512]{1,0:T(2,128)S(1)}, s32[2]{0:T(128)S(1)}, f32[1024]{0:T(1024)S(1)}, bf16[1024,1024]{1,0:T(8,128)(2,1)}, /*index=5*/s32[]{:T(128)}, s32[1]{0:T(128)}, s32[]{:T(128)}, s32[]{:T(128)}) while((s32[]{:T(128)}, f32[2,512]{1,0:T(2,128)S(1)}, s32[2]{0:T(128)S(1)}, f32[1024]{0:T(1024)S(1)}, ...), condition=%wide.region_8.9_spmd.clone, body=%wide.region_6.8_spmd.clone.sunk | while | flops 1076888576 | bytes 3172527 | solution.py:49
  97.0 0.6 dynamic_slice.19
  98.2 0.1 dynamic_slice.20
  98.3 3.6 %select_reduce_fusion.2 = f32[512]{0:T(512)S(1)} fusion(bf16[1024,1024]{1,0:T(8,128)(2,1)} %get-tuple-element.114, s32[]{:T(128)S(6)} %select_n.45, s32[512]{0:T(512)S(1)} %iota_add_fusion.2, f32[1024]{0:T(1024)S(1)} %get-tuple-element.113, f32[512]{0:T(512)S(1)} %dynamic_slice.20, pred[1024]{0:T(1024)(128)(4,1)S(1)} %broadcast_compare_fusion.3), kind=kOutput, calls=%fused_computation.5.clone.1 | convolution fusion | flops 1076887040 | bytes 3156996 | tf_op jit(solution)/shard_map/while/body/eval_jaxpr/dot_general | solution.py:15
  102.0 0.6 dynamic_slice.19
  103.2 0.1 dynamic_slice.20
  103.3 3.6 %select_reduce_fusion.2 = f32[512]{0:T(512)S(1)} fusion(bf16[1024,1024]{1,0:T(8,128)(2,1)} %get-tuple-element.114, s32[]{:T(128)S(6)} %select_n.45, s32[512]{0:T(512)S(1)} %iota_add_fusion.2, f32[1024]{0:T(1024)S(1)} %get-tuple-element.113, f32[512]{0:T(512)S(1)} %dynamic_slice.20, pred[1024]{0:T(1024)(128)(4,1)S(1)} %broadcast_compare_fusion.3), kind=kOutput, calls=%fused_computation.5.clone.1 | convolution fusion | flops 1076887040 | bytes 3156996 | tf_op jit(solution)/shard_map/while/body/eval_jaxpr/dot_general | solution.py:15
  106.9 0.7 all_to_all.18
  107.7 4.5 %all-to-all-start.2 = ((f32[128,1,8]{2,1,0:T(1,128)}), f32[128,1,8]{2,1,0:T(1,128)S(1)}, u32[]{:S(2)}, u32[]{:S(2)}) async-start(f32[128,1,8]{2,1,0:T(1,128)} %bitcast.2), calls=%async_computation.2 | async-start | bytes 131072 | tf_op jit(solution)/shard_map/all_to_all | solution.py:91
  112.2 9.9 %all-to-all-done.2 = f32[128,1,8]{2,1,0:T(1,128)S(1)} async-done(((f32[128,1,8]{2,1,0:T(1,128)}), f32[128,1,8]{2,1,0:T(1,128)S(1)}, u32[]{:S(2)}, u32[]{:S(2)}) %all-to-all-start.2) | async-done | bytes 4128 | tf_op jit(solution)/shard_map/all_to_all | solution.py:91
  122.2 0.5 broadcast.69
  122.7 0.8 reduce.7
  123.5 0.1 reshape.53
  123.6 3.4 %gather_fusion = f32[512]{0:T(512)} fusion(f32[1024]{0:T(1024)S(1)} %reshape.53, s32[1024]{0:T(1024)S(1)} %pad_clamp_fusion), kind=kCustom, calls=%fused_computation | custom fusion | bytes 6144 | tf_op jit(solution)/shard_map/gather | solution.py:94
  127.0 83.6 %all-gather.2.cloned.1.call-done = bf16[16384,1024]{1,0:T(8,128)(2,1)} async-done(((bf16[1024,1024]{1,0:T(8,128)(2,1)}), bf16[16384,1024]{1,0:T(8,128)(2,1)}) %all-gather.2.cloned.1.call-update) | async-done | bytes 33554448 | tf_op jit(solution)/shard_map/all_gather | solution.py:63
  210.6 28.6 %multiply_reduce_fusion = (f32[512]{0:T(512)S(1)}, f32[512,16384]{1,0:T(8,128)}) fusion(bf16[16384,1024]{1,0:T(8,128)(2,1)} %all-gather.2.cloned.1.call-done, f32[512,1024]{1,0:T(8,128)S(1)} %copy-done.1, f32[512]{0:T(512)S(1)} %add_rsqrt_fusion.1), kind=kOutput, calls=%fused_computation.12 | convolution fusion | flops 17197694976 | bytes 69210112 | tf_op jit(solution)/shard_map/dot_general | solution.py:15
  239.2 14.1 %exponential_reduce_fusion = f32[512]{0:T(512)S(1)} fusion(f32[512,16384]{1,0:T(8,128)} %get-tuple-element.60, f32[512]{0:T(512)S(1)} %get-tuple-element.59), kind=kLoop, calls=%fused_computation.11 | loop fusion | flops 25165312 | bytes 33558528 | tf_op jit(solution)/shard_map/reduce_sum | solution.py:23
  253.3 0.6 fusion.11
  (12 shorter events, 0.1 us)
Async XLA Ops:
  7.2 203.4 %all-gather.2.cloned.1.call-start = ((), (), s32[]{:S(2)}) async-start(), calls=%async_computation.3 | async-start | bytes 35651584 | tf_op jit(solution)/shard_map/all_gather | solution.py:63
  7.2 3.5 %copy-start = (f32[1024,1024]{1,0:T(8,128)S(1)}, f32[1024,1024]{1,0:T(8,128)}, u32[]{:S(2)}) copy-start(f32[1024,1024]{1,0:T(8,128)} %param.7) | copy-start | bytes 12582916
  10.7 1.6 copy-start.3
  12.3 0.7 copy-start.2
  12.3 16.7 %copy-start.1 = (f32[512,1024]{1,0:T(8,128)S(1)}, f32[512,1024]{1,0:T(8,128)}, u32[]{:S(2)}) copy-start(f32[512,1024]{1,0:T(8,128)} %param.6) | copy-start | bytes 6291460
  17.5 21.3 %all-to-all-start = ((bf16[128,1,8]{2,1,0:T(2,128)(2,1)}), bf16[128,1,8]{2,1,0:T(2,128)(2,1)S(1)}, u32[]{:S(2)}, u32[]{:S(2)}) async-start(bf16[128,1,8]{2,1,0:T(2,128)(2,1)} %all_to_all.20), calls=%async_computation | async-start | bytes 131072 | tf_op jit(solution)/shard_map/all_to_all | solution.py:79
  38.8 58.1 %all-to-all-start.1 = ((bf16[128,8,1024]{2,1,0:T(8,128)(2,1)}), bf16[128,8,1024]{2,1,0:T(8,128)(2,1)}, u32[]{:S(2)}, u32[]{:S(2)}) async-start(bf16[128,8,1024]{2,1,0:T(8,128)(2,1)} %bitcast.13), calls=%async_computation.1 | async-start | bytes 4194304 | tf_op jit(solution)/shard_map/all_to_all | solution.py:72
  107.7 14.5 %all-to-all-start.2 = ((f32[128,1,8]{2,1,0:T(1,128)}), f32[128,1,8]{2,1,0:T(1,128)S(1)}, u32[]{:S(2)}, u32[]{:S(2)}) async-start(f32[128,1,8]{2,1,0:T(1,128)} %bitcast.2), calls=%async_computation.2 | async-start | bytes 131072 | tf_op jit(solution)/shard_map/all_to_all | solution.py:91
Sparse Core Ops, SparseCore 0:
  12.4 198.1 all-gather.1
where the time goes:
time: 261 us
  waiting for transfers between devices  151 us (58%)
  matrix products  35.8 us (14%)
  other arithmetic  24.4 us (9%)
  starting transfers between devices  21.4 us (8%)
  between operations  14.1 us (5%)
  local copies, waits for them, and re-layouts  12.2 us (5%)
    all_gather x1, waiting for transfers between devices, per_device(): lax.all_gather(centre, 'cent', axis=0, tiled=True)  83.6 us
    all_to_all x1, waiting for transfers between devices, per_device(): lax.all_to_all(send_rows.reshape(devices, capacity, width), ('doc', 'cent...  52.5 us
    dot_general x3, matrix products, inner_rows(): lax.dot_general(left, right, (((1,), (1,)), ((), ())), preferred_element_...  35.8 us
    reduce_sum x1, other arithmetic, block_terms(): return (high, jnp.sum(jnp.exp(score - high[:, None]), axis=1))  14.1 us
    all_to_all x1, starting transfers between devices, per_device(): lax.all_to_all(send_ids.reshape(devices, capacity), ('doc', 'cent'), spli...  11.5 us
    all_to_all x1, waiting for transfers between devices, per_device(): lax.all_to_all(best.reshape(devices, capacity), ('doc', 'cent'), split_ax...  9.95 us
    all_to_all x1, waiting for transfers between devices, per_device(): lax.all_to_all(send_ids.reshape(devices, capacity), ('doc', 'cent'), spli...  5.37 us
    all_to_all x1, starting transfers between devices, per_device(): lax.all_to_all(send_rows.reshape(devices, capacity, width), ('doc', 'cent...  5.32 us
  transfers between devices with their start and end apart: 4, of which 4 were waited for; matrix products, arithmetic and copies ran while one was open for 8% of the time, Pallas kernels for 0%

commit v1 on v0

--- a/solution.py
+++ b/solution.py
@@ -60,7 +60,13 @@
     centre = unit_rows(centroids)
     start_terms = (jnp.full((row_count,), -1e30, jnp.float32), jnp.zeros((row_count,), jnp.float32))
     high, total = join_terms(
-        start_terms, block_terms(unit, lax.all_gather(centre, "cent", axis=0, tiled=True))
+        start_terms,
+        block_terms(
+            unit,
+            jnp.concatenate(
+                lax.all_to_all(jnp.stack([centre] * lax.axis_size("cent")), "cent", 0, 0), axis=0
+            ),
+        ),
     )
     soft_cost = 1.0 - (high + jnp.log(total)) / inverse_temp
     owner = cluster // per_owner

time: 261 us -> 516 us (1.98)
  waiting for transfers between devices: 151 us -> 397 us
  between operations: 14.1 us -> 0.73 us
  local copies, waits for them, and re-layouts: 12.2 us -> 22.9 us
  starting transfers between devices: 21.4 us -> 28.8 us
    all_to_all x0 -> x1, waiting for transfers between devices: none -> 360 us  [per_device(): lax.all_to_all(jnp.stack([centre] * lax.axis_size('cent')), 'cent', 0, 0)]
    all_gather x1 -> x0, waiting for transfers between devices: 83.6 us -> none  [per_device(): lax.all_gather(centre, 'cent', axis=0, tiled=True)]
    all_to_all x1, waiting for transfers between devices: 52.5 us -> 27.1 us  [per_device(): lax.all_to_all(send_rows.reshape(devices, capacity, width), ('doc', 'cent...]
    another operation x0 -> x1, local copies, waits for them, and re-layouts: none -> 12.2 us  [per_device(): jnp.stack([centre] * lax.axis_size('cent'))]
    all_to_all x0 -> x1, starting transfers between devices: none -> 6.31 us  [per_device(): lax.all_to_all(jnp.stack([centre] * lax.axis_size('cent')), 'cent', 0, 0)]
  transfers between devices with their start and end apart: 4 -> 4, of which waited for: 4 -> 4; matrix products, arithmetic and copies ran while one was open for 8% -> 3% of each run, Pallas kernels for 0% -> 0%
where the time goes in v1:
time: 516 us; the launch traced here: 515 us
  waiting for transfers between devices  397 us (77%)
  matrix products  35.8 us (7%)
  other arithmetic  28.9 us (6%)
  starting transfers between devices  28.8 us (6%)
  local copies, waits for them, and re-layouts  22.9 us (4%)
    all_to_all x1, waiting for transfers between devices, per_device(): lax.all_to_all(jnp.stack([centre] * lax.axis_size('cent')), 'cent', 0, 0)  360 us
    dot_general x3, matrix products, inner_rows(): lax.dot_general(left, right, (((1,), (1,)), ((), ())), preferred_element_...  35.8 us
    all_to_all x1, waiting for transfers between devices, per_device(): lax.all_to_all(send_rows.reshape(devices, capacity, width), ('doc', 'cent...  27.1 us
    reduce_sum x1, other arithmetic, block_terms(): return (high, jnp.sum(jnp.exp(score - high[:, None]), axis=1))  14.1 us
    another operation x1, local copies, waits for them, and re-layouts, per_device(): jnp.stack([centre] * lax.axis_size('cent'))  12.2 us
    all_to_all x1, starting transfers between devices, per_device(): lax.all_to_all(send_ids.reshape(devices, capacity), ('doc', 'cent'), spli...  11.5 us
  transfers between devices with their start and end apart: 4, of which 4 were waited for; matrix products, arithmetic and copies ran while one was open for 3% of the time, Pallas kernels for 0%

profile of v1, /device:TPU:1, one launch (start us, length us, event | category | flops | bytes accessed | tf_op | source)
XLA Modules:
  0.0 515.0 jit_solution(18246347704172117958)
XLA Ops:
  0.6 0.0 copy-start
  0.6 0.9 fusion.14
  1.5 3.8 scatter_custom_fusion
  5.3 0.7 all_to_all.24
  6.0 11.5 %all-to-all-start.1 = ((bf16[128,1,8]{2,1,0:T(2,128)(2,1)}), bf16[128,1,8]{2,1,0:T(2,128)(2,1)S(1)}, u32[]{:S(2)}, u32[]{:S(2)}) async-start(bf16[128,1,8]{2,1,0:T(2,128)(2,1)} %all_to_all.24), calls=%async_computation.1 | async-start | bytes 131072 | tf_op jit(solution)/shard_map/all_to_all | solution.py:85
  17.5 1.8 multiply_reduce_fusion.2
  19.3 0.0 copy-done
  19.3 4.2 scatter_custom_fusion.1
  23.6 3.8 all-to-all-done.1
  27.3 6.5 %all-to-all-start.2 = ((bf16[128,8,1024]{2,1,0:T(8,128)(2,1)}), bf16[128,8,1024]{2,1,0:T(8,128)(2,1)}, u32[]{:S(2)}, u32[]{:S(2)}) async-start(bf16[128,8,1024]{2,1,0:T(8,128)(2,1)} %bitcast.14), calls=%async_computation.2 | async-start | bytes 4194304 | tf_op jit(solution)/shard_map/all_to_all | solution.py:78
  33.8 2.5 multiply_reduce_fusion.1
  36.3 0.2 convert_reduce_fusion
  36.5 0.1 reshape.60
  36.6 27.1 %all-to-all-done.2 = bf16[128,8,1024]{2,1,0:T(8,128)(2,1)} async-done(((bf16[128,8,1024]{2,1,0:T(8,128)(2,1)}), bf16[128,8,1024]{2,1,0:T(8,128)(2,1)}, u32[]{:S(2)}, u32[]{:S(2)}) %all-to-all-start.2) | async-done | bytes 2097184 | tf_op jit(solution)/shard_map/all_to_all | solution.py:78
  63.7 9.9 %while.11 = (s32[]{:T(128)}, f32[2,512]{1,0:T(2,128)S(1)}, s32[2]{0:T(128)S(1)}, f32[1024]{0:T(1024)S(1)}, bf16[1024,1024]{1,0:T(8,128)(2,1)}, /*index=5*/s32[]{:T(128)}, s32[1]{0:T(128)}, s32[]{:T(128)}, s32[]{:T(128)}) while((s32[]{:T(128)}, f32[2,512]{1,0:T(2,128)S(1)}, s32[2]{0:T(128)S(1)}, f32[1024]{0:T(1024)S(1)}, ...), condition=%wide.region_8.9_spmd.clone, body=%wide.region_6.8_spmd.clone.sunk | while | flops 1076888576 | bytes 3172527 | solution.py:49
  63.7 0.6 dynamic_slice.19
  65.0 0.1 dynamic_slice.20
  65.1 3.6 select_reduce_fusion.2
  68.7 0.6 dynamic_slice.19
  69.9 0.1 dynamic_slice.20
  70.0 3.6 select_reduce_fusion.2
  73.7 0.7 all_to_all.22
  74.4 4.5 all-to-all-start.3
  78.9 3.8 multiply_convert_fusion
  82.7 6.1 %all-to-all-done.3 = f32[128,1,8]{2,1,0:T(1,128)S(1)} async-done(((f32[128,1,8]{2,1,0:T(1,128)}), f32[128,1,8]{2,1,0:T(1,128)S(1)}, u32[]{:S(2)}, u32[]{:S(2)}) %all-to-all-start.3) | async-done | bytes 4128 | tf_op jit(solution)/shard_map/all_to_all | solution.py:97
  88.8 12.2 %stack.2 = bf16[16,1024,1024]{2,1,0:T(8,128)(2,1)} broadcast(bf16[1024,1024]{1,0:T(8,128)(2,1)} %multiply_convert_fusion), dimensions={1,2} | broadcast | bytes 35651584 | tf_op jit(solution)/shard_map/stack | solution.py:67
  101.0 6.3 %all-to-all-start = ((bf16[16,1024,1024]{2,1,0:T(8,128)(2,1)}), bf16[16,1024,1024]{2,1,0:T(8,128)(2,1)}, u32[]{:S(2)}, u32[]{:S(2)}) async-start(bf16[16,1024,1024]{2,1,0:T(8,128)(2,1)} %stack.2), calls=%async_computation | async-start | bytes 67108864 | tf_op jit(solution)/shard_map/all_to_all | solution.py:67
  107.3 0.5 broadcast.71
  107.8 0.8 reduce.7
  108.7 0.1 reshape.59
  108.7 3.4 gather_fusion
  112.2 359.5 %all-to-all-done = bf16[16,1024,1024]{2,1,0:T(8,128)(2,1)} async-done(((bf16[16,1024,1024]{2,1,0:T(8,128)(2,1)}), bf16[16,1024,1024]{2,1,0:T(8,128)(2,1)}, u32[]{:S(2)}, u32[]{:S(2)}) %all-to-all-start) | async-done | bytes 33554464 | tf_op jit(solution)/shard_map/all_to_all | solution.py:67
  471.7 28.6 %multiply_reduce_fusion = (f32[512]{0:T(512)S(1)}, f32[512,16384]{1,0:T(8,128)}) fusion(bf16[16384,1024]{1,0:T(8,128)(2,1)} %bitcast, f32[512,1024]{1,0:T(8,128)S(1)} %copy-done, f32[512]{0:T(512)S(1)} %add_rsqrt_fusion.1), kind=kOutput, calls=%fused_computation.12 | convolution fusion | flops 17197694976 | bytes 69210112 | tf_op jit(solution)/shard_map/dot_general | solution.py:15
  500.3 14.1 %exponential_reduce_fusion = f32[512]{0:T(512)S(1)} fusion(f32[512,16384]{1,0:T(8,128)} %get-tuple-element.60, f32[512]{0:T(512)S(1)} %get-tuple-element.59), kind=kLoop, calls=%fused_computation.11 | loop fusion | flops 25165312 | bytes 33558528 | tf_op jit(solution)/shard_map/reduce_sum | solution.py:23
  514.4 0.6 fusion.11
  (11 shorter events, 0.1 us)
Async XLA Ops:
  0.6 18.7 %copy-start = (f32[512,1024]{1,0:T(8,128)S(1)}, f32[512,1024]{1,0:T(8,128)}, u32[]{:S(2)}) copy-start(f32[512,1024]{1,0:T(8,128)} %param.6) | copy-start | bytes 6291460
  6.0 21.3 %all-to-all-start.1 = ((bf16[128,1,8]{2,1,0:T(2,128)(2,1)}), bf16[128,1,8]{2,1,0:T(2,128)(2,1)S(1)}, u32[]{:S(2)}, u32[]{:S(2)}) async-start(bf16[128,1,8]{2,1,0:T(2,128)(2,1)} %all_to_all.24), calls=%async_computation.1 | async-start | bytes 131072 | tf_op jit(solution)/shard_map/all_to_all | solution.py:85
  27.3 36.4 %all-to-all-start.2 = ((bf16[128,8,1024]{2,1,0:T(8,128)(2,1)}), bf16[128,8,1024]{2,1,0:T(8,128)(2,1)}, u32[]{:S(2)}, u32[]{:S(2)}) async-start(bf16[128,8,1024]{2,1,0:T(8,128)(2,1)} %bitcast.14), calls=%async_computation.2 | async-start | bytes 4194304 | tf_op jit(solution)/shard_map/all_to_all | solution.py:78
  74.4 14.5 %all-to-all-start.3 = ((f32[128,1,8]{2,1,0:T(1,128)}), f32[128,1,8]{2,1,0:T(1,128)S(1)}, u32[]{:S(2)}, u32[]{:S(2)}) async-start(f32[128,1,8]{2,1,0:T(1,128)} %bitcast.3), calls=%async_computation.3 | async-start | bytes 131072 | tf_op jit(solution)/shard_map/all_to_all | solution.py:97
  101.0 370.7 %all-to-all-start = ((bf16[16,1024,1024]{2,1,0:T(8,128)(2,1)}), bf16[16,1024,1024]{2,1,0:T(8,128)(2,1)}, u32[]{:S(2)}, u32[]{:S(2)}) async-start(bf16[16,1024,1024]{2,1,0:T(8,128)(2,1)} %stack.2), calls=%async_computation | async-start | bytes 67108864 | tf_op jit(solution)/shard_map/all_to_all | solution.py:67
